TPU v7x, 32 devices: a whole 2x2x4 slice. The times are simulated.
32 devices in a mesh: section: 4 (over z), seq: 8 (over y, x, core).
Axes of the slice: x: 2, y: 2, z: 4, core: 2. Of those that a mesh axis runs over, the one named last changes fastest.
Arguments:
- bases: int32 [4, 262144], P(None, 'seq'), may hold values from 0 to 3
- stem_weight: bfloat16 [512, 1536], replicated, may hold values from -0.5 to 0.5
- norm_gain: float32 [4, 1536], P('section'), may hold values from 0.25 to 1.75
- conv_taps: float32 [4, 5, 1536], P('section'), may hold values from -2.7 to 2.7
- proj_weight: bfloat16 [4, 1536, 1536], P('section'), may hold values from -0.15625 to 0.15625
- dest: int32 [256], P('seq'), may hold values from 0 to 255, as said below
Outputs:
- hints: bfloat16 [4, 4, 2048, 1536], P('section', None, 'seq')
Inputs may be any that keep to these rules, and one draw needn't show every extreme that they name: dest is a permutation. Slot dest[r] belongs to owner dest[r] // 32; the runs of one index d of seq (r from d * 32) go to every owner in equal numbers, 4 each, and (dest[r] % 32) // 4 equals d.
All inputs are finite; a program needn't handle non-finite values.
Results may differ from a plain program's by a relative error of at most 0.007.
Values may be sent and summed in bfloat16 or wider, within the bound.
A program may use at most 64 MiB of HBM per device.

v0:
```python
import jax
import jax.numpy as jnp
from jax import lax
from jax.sharding import PartitionSpec as P

BLOCK_BP = 128


def extended(block, sides, width):
    for axis, dim in sides:
        count = lax.axis_size(axis)
        forward = [(i, i + 1) for i in range(count - 1)]
        backward = [(target, source) for source, target in forward]
        low = lax.ppermute(
            lax.slice_in_dim(block, block.shape[dim] - width, None, axis=dim), axis, forward
        )
        high = lax.ppermute(lax.slice_in_dim(block, 0, width, axis=dim), axis, backward)
        block = jnp.concatenate([low, block, high], axis=dim)
    return block


def passed_along(value, axis, steps):
    count = lax.axis_size(axis)
    initial, last = (max(0, -steps), min(count, count - steps))
    return lax.ppermute(value, axis, [(source, source + steps) for source in range(initial, last)])


def section_block(current, gain_row, tap_rows, weight):
    wide_state = current.astype(jnp.float32)
    inv_rms = lax.rsqrt(jnp.mean(wide_state * wide_state, axis=-1, keepdims=True) + 1e-06)
    normed = (wide_state * inv_rms * gain_row).astype(jnp.bfloat16)
    reach = tap_rows.shape[0] // 2
    padded = extended(normed, (("seq", 0),), reach)
    length = current.shape[0]
    mixed = jnp.zeros(current.shape, jnp.float32)
    for offset in range(tap_rows.shape[0]):
        mixed = mixed + tap_rows[offset] * padded[offset : offset + length].astype(jnp.float32)
    mixed = mixed.astype(jnp.bfloat16)
    update = jnp.dot(mixed, weight, preferred_element_type=jnp.float32)
    return (wide_state + jax.nn.gelu(update)).astype(jnp.bfloat16)


def on_device(bases, stem_weight, norm_gain, conv_taps, proj_weight, dest):
    micro_count = bases.shape[0]
    row_count = bases.shape[1] // BLOCK_BP
    channels = stem_weight.shape[1]
    section_count = lax.axis_size("section")
    section_id = lax.axis_index("section")
    segs_dev = dest.shape[0]
    per_peer = segs_dev // lax.axis_size("seq")
    seg_rows = row_count // segs_dev
    base_codes = bases.reshape(micro_count * row_count, BLOCK_BP)
    onehot = (base_codes[:, :, None] == jnp.arange(4, dtype=jnp.int32)).astype(jnp.bfloat16)
    onehot = onehot.reshape(micro_count * row_count, BLOCK_BP * 4)
    embedded = jnp.dot(onehot, stem_weight, preferred_element_type=jnp.float32).astype(jnp.bfloat16)
    embedded = embedded.reshape(micro_count, row_count, channels)
    gain_row = norm_gain[0]
    tap_rows = conv_taps[0]
    weight = proj_weight[0]
    send_slot = dest // segs_dev * per_peer + dest % segs_dev % per_peer
    select = (send_slot[None, :] == jnp.arange(segs_dev, dtype=jnp.int32)[:, None]).astype(
        jnp.bfloat16
    )

    def arrange(current):
        grouped = current.reshape(segs_dev, seg_rows * channels)
        ordered = jnp.dot(select, grouped, preferred_element_type=jnp.float32).astype(jnp.bfloat16)
        return ordered.reshape(row_count, channels)

    def advance(moment, carried):
        incoming, hint_rows = carried
        entering = lax.dynamic_index_in_dim(
            embedded, jnp.clip(moment, 0, micro_count - 1), 0, keepdims=False
        )
        current = jnp.where(section_id == 0, entering, incoming)
        leaving = section_block(current, gain_row, tap_rows, weight)
        micro_idx = moment - section_id
        slot_idx = jnp.clip(micro_idx, 0, micro_count - 1)
        in_range = (micro_idx >= 0) & (micro_idx < micro_count)
        arrived = lax.all_to_all(arrange(leaving), "seq", split_axis=0, concat_axis=0, tiled=True)
        previous = lax.dynamic_index_in_dim(hint_rows, slot_idx, 0, keepdims=False)
        arrived = jnp.where(in_range, arrived, previous)
        hint_rows = lax.dynamic_update_index_in_dim(hint_rows, arrived, slot_idx, 0)
        incoming = passed_along(leaving, "section", 1)
        return (incoming, hint_rows)

    start_state = jnp.zeros((row_count, channels), jnp.bfloat16)
    start_hints = jnp.zeros((micro_count, row_count, channels), jnp.bfloat16)
    final_state, hint_rows = lax.fori_loop(
        0, micro_count + section_count - 1, advance, (start_state, start_hints)
    )
    return hint_rows[None]


def solution(mesh):
    return jax.shard_map(
        on_device,
        mesh=mesh,
        in_specs=(
            P(None, "seq"),
            P(),
            P("section", None),
            P("section", None, None),
            P("section", None, None),
            P("seq"),
        ),
        out_specs=P("section", None, "seq", None),
        check_vma=False,
    )
```

profile of v0, /device:TPU:25, one launch (start us, length us, event | category | flops | bytes accessed | tf_op | source)
XLA Modules:
  0.0 319.5 jit_solution(564011685951406488)
XLA Ops:
  8.2 5.2 %convolution_convert_fusion.1 = bf16[1024,1536]{1,0:T(8,128)(2,1)} fusion(bf16[512,1536]{1,0:T(8,128)(2,1)S(1)} %copy-done, s32[1024,512]{0,1:T(8,128)} %eq.50, s32[512]{0:T(512)S(1)} %eq.52), kind=kOutput, calls=%fused_computation.48 | convolution fusion | flops 1612709888 | bytes 6817792 | tf_op jit(solution)/shard_map/dot_general | solution.py:55
  15.3 304.2 %while.17 = (s32[]{:T(128)}, bf16[256,1536]{1,0:T(8,128)(2,1)S(1)}, bf16[4,256,1536]{2,1,0:T(8,128)(2,1)}, pred[]{:T(512)}, bf16[4,256,1536]{2,1,0:T(8,128)(2,1)...) while((s32[]{:T(128)}, bf16[256,1536]{1,0:T(8,128)(2,1)S(1)}, ...), condition=%wide.region_2.3_spmd.clone, body=%wide.region_0.2_spmd.clone.sunk | while | flops 1252002048 | bytes 23794180 | solution.py:89
  23.5 5.4 %fusion.52 = bf16[256,1536]{1,0:T(8,128)(2,1)} fusion(bf16[256,1536]{1,0:T(8,128)(2,1)S(1)} %get-tuple-element.323, bf16[1536,1536]{1,0:T(8,128)(2,1)} %get-tuple-element.369, bf16[256,1536]{1,0:T(8,128)(2,1)S(1)} %fusion.50, bf16[2,1536]{1,0:T(2,128)(2,1)S(1)} %collective-permute-done, bf16[2,1536]{1,0:T(2,128)(2,1)S(1)} %collective-permute-done.1, ...), kind=kOutput, calls=%fused_computation.10.clone.1 | convolution fusion | flops 1222901760 | bytes 7120896 | tf_op jit(solution)/shard_map/while/body/eval_jaxpr/dot_general | solution.py:39
  32.0 5.8 %all-to-all-start = ((bf16[8,32,1536]{2,1,0:T(8,128)(2,1)}), bf16[8,32,1536]{2,1,0:T(8,128)(2,1)S(1)}, u32[]{:S(2)}, u32[]{:S(2)}) async-start(bf16[8,32,1536]{2,1,0:T(8,128)(2,1)} %all_to_all.18), calls=%async_computation | async-start | bytes 1572864 | tf_op jit(solution)/shard_map/while/body/eval_jaxpr/all_to_all | solution.py:80
  39.0 7.8 %all-to-all-done = bf16[8,32,1536]{2,1,0:T(8,128)(2,1)S(1)} async-done(((bf16[8,32,1536]{2,1,0:T(8,128)(2,1)}), bf16[8,32,1536]{2,1,0:T(8,128)(2,1)S(1)}, u32[]{:S(2)}, u32[]{:S(2)}) %all-to-all-start) | async-done | bytes 786464 | tf_op jit(solution)/shard_map/while/body/eval_jaxpr/all_to_all | solution.py:80
  49.0 9.9 %collective-permute-done.2 = bf16[256,1536]{1,0:T(8,128)(2,1)S(1)} collective-permute-done((bf16[256,1536]{1,0:T(8,128)(2,1)}, bf16[256,1536]{1,0:T(8,128)(2,1)S(1)}, u32[]{:S(2)}, u32[]{:S(2)}) %collective-permute-start.2) | collective-permute-done | bytes 786464 | tf_op jit(solution)/shard_map/while/body/eval_jaxpr/ppermute | solution.py:25
  63.5 3.2 collective-permute-start.1
  67.4 5.4 %fusion.52 = bf16[256,1536]{1,0:T(8,128)(2,1)} fusion(bf16[256,1536]{1,0:T(8,128)(2,1)S(1)} %get-tuple-element.323, bf16[1536,1536]{1,0:T(8,128)(2,1)} %get-tuple-element.369, bf16[256,1536]{1,0:T(8,128)(2,1)S(1)} %fusion.50, bf16[2,1536]{1,0:T(2,128)(2,1)S(1)} %collective-permute-done, bf16[2,1536]{1,0:T(2,128)(2,1)S(1)} %collective-permute-done.1, ...), kind=kOutput, calls=%fused_computation.10.clone.1 | convolution fusion | flops 1222901760 | bytes 7120896 | tf_op jit(solution)/shard_map/while/body/eval_jaxpr/dot_general | solution.py:39
  75.9 5.2 %all-to-all-start = ((bf16[8,32,1536]{2,1,0:T(8,128)(2,1)}), bf16[8,32,1536]{2,1,0:T(8,128)(2,1)S(1)}, u32[]{:S(2)}, u32[]{:S(2)}) async-start(bf16[8,32,1536]{2,1,0:T(8,128)(2,1)} %all_to_all.18), calls=%async_computation | async-start | bytes 1572864 | tf_op jit(solution)/shard_map/while/body/eval_jaxpr/all_to_all | solution.py:80
  82.4 7.8 %all-to-all-done = bf16[8,32,1536]{2,1,0:T(8,128)(2,1)S(1)} async-done(((bf16[8,32,1536]{2,1,0:T(8,128)(2,1)}), bf16[8,32,1536]{2,1,0:T(8,128)(2,1)S(1)}, u32[]{:S(2)}, u32[]{:S(2)}) %all-to-all-start) | async-done | bytes 786464 | tf_op jit(solution)/shard_map/while/body/eval_jaxpr/all_to_all | solution.py:80
  92.5 9.9 %collective-permute-done.2 = bf16[256,1536]{1,0:T(8,128)(2,1)S(1)} collective-permute-done((bf16[256,1536]{1,0:T(8,128)(2,1)}, bf16[256,1536]{1,0:T(8,128)(2,1)S(1)}, u32[]{:S(2)}, u32[]{:S(2)}) %collective-permute-start.2) | collective-permute-done | bytes 786464 | tf_op jit(solution)/shard_map/while/body/eval_jaxpr/ppermute | solution.py:25
  106.9 3.2 collective-permute-start.1
  110.9 5.4 %fusion.52 = bf16[256,1536]{1,0:T(8,128)(2,1)} fusion(bf16[256,1536]{1,0:T(8,128)(2,1)S(1)} %get-tuple-element.323, bf16[1536,1536]{1,0:T(8,128)(2,1)} %get-tuple-element.369, bf16[256,1536]{1,0:T(8,128)(2,1)S(1)} %fusion.50, bf16[2,1536]{1,0:T(2,128)(2,1)S(1)} %collective-permute-done, bf16[2,1536]{1,0:T(2,128)(2,1)S(1)} %collective-permute-done.1, ...), kind=kOutput, calls=%fused_computation.10.clone.1 | convolution fusion | flops 1222901760 | bytes 7120896 | tf_op jit(solution)/shard_map/while/body/eval_jaxpr/dot_general | solution.py:39
  119.3 5.2 %all-to-all-start = ((bf16[8,32,1536]{2,1,0:T(8,128)(2,1)}), bf16[8,32,1536]{2,1,0:T(8,128)(2,1)S(1)}, u32[]{:S(2)}, u32[]{:S(2)}) async-start(bf16[8,32,1536]{2,1,0:T(8,128)(2,1)} %all_to_all.18), calls=%async_computation | async-start | bytes 1572864 | tf_op jit(solution)/shard_map/while/body/eval_jaxpr/all_to_all | solution.py:80
  125.9 7.8 %all-to-all-done = bf16[8,32,1536]{2,1,0:T(8,128)(2,1)S(1)} async-done(((bf16[8,32,1536]{2,1,0:T(8,128)(2,1)}), bf16[8,32,1536]{2,1,0:T(8,128)(2,1)S(1)}, u32[]{:S(2)}, u32[]{:S(2)}) %all-to-all-start) | async-done | bytes 786464 | tf_op jit(solution)/shard_map/while/body/eval_jaxpr/all_to_all | solution.py:80
  135.9 9.9 %collective-permute-done.2 = bf16[256,1536]{1,0:T(8,128)(2,1)S(1)} collective-permute-done((bf16[256,1536]{1,0:T(8,128)(2,1)}, bf16[256,1536]{1,0:T(8,128)(2,1)S(1)}, u32[]{:S(2)}, u32[]{:S(2)}) %collective-permute-start.2) | collective-permute-done | bytes 786464 | tf_op jit(solution)/shard_map/while/body/eval_jaxpr/ppermute | solution.py:25
  154.3 5.4 %fusion.52 = bf16[256,1536]{1,0:T(8,128)(2,1)} fusion(bf16[256,1536]{1,0:T(8,128)(2,1)S(1)} %get-tuple-element.323, bf16[1536,1536]{1,0:T(8,128)(2,1)} %get-tuple-element.369, bf16[256,1536]{1,0:T(8,128)(2,1)S(1)} %fusion.50, bf16[2,1536]{1,0:T(2,128)(2,1)S(1)} %collective-permute-done, bf16[2,1536]{1,0:T(2,128)(2,1)S(1)} %collective-permute-done.1, ...), kind=kOutput, calls=%fused_computation.10.clone.1 | convolution fusion | flops 1222901760 | bytes 7120896 | tf_op jit(solution)/shard_map/while/body/eval_jaxpr/dot_general | solution.py:39
  162.7 5.2 %all-to-all-start = ((bf16[8,32,1536]{2,1,0:T(8,128)(2,1)}), bf16[8,32,1536]{2,1,0:T(8,128)(2,1)S(1)}, u32[]{:S(2)}, u32[]{:S(2)}) async-start(bf16[8,32,1536]{2,1,0:T(8,128)(2,1)} %all_to_all.18), calls=%async_computation | async-start | bytes 1572864 | tf_op jit(solution)/shard_map/while/body/eval_jaxpr/all_to_all | solution.py:80
  169.3 7.8 %all-to-all-done = bf16[8,32,1536]{2,1,0:T(8,128)(2,1)S(1)} async-done(((bf16[8,32,1536]{2,1,0:T(8,128)(2,1)}), bf16[8,32,1536]{2,1,0:T(8,128)(2,1)S(1)}, u32[]{:S(2)}, u32[]{:S(2)}) %all-to-all-start) | async-done | bytes 786464 | tf_op jit(solution)/shard_map/while/body/eval_jaxpr/all_to_all | solution.py:80
  179.3 9.9 %collective-permute-done.2 = bf16[256,1536]{1,0:T(8,128)(2,1)S(1)} collective-permute-done((bf16[256,1536]{1,0:T(8,128)(2,1)}, bf16[256,1536]{1,0:T(8,128)(2,1)S(1)}, u32[]{:S(2)}, u32[]{:S(2)}) %collective-permute-start.2) | collective-permute-done | bytes 786464 | tf_op jit(solution)/shard_map/while/body/eval_jaxpr/ppermute | solution.py:25
  197.7 5.4 %fusion.52 = bf16[256,1536]{1,0:T(8,128)(2,1)} fusion(bf16[256,1536]{1,0:T(8,128)(2,1)S(1)} %get-tuple-element.323, bf16[1536,1536]{1,0:T(8,128)(2,1)} %get-tuple-element.369, bf16[256,1536]{1,0:T(8,128)(2,1)S(1)} %fusion.50, bf16[2,1536]{1,0:T(2,128)(2,1)S(1)} %collective-permute-done, bf16[2,1536]{1,0:T(2,128)(2,1)S(1)} %collective-permute-done.1, ...), kind=kOutput, calls=%fused_computation.10.clone.1 | convolution fusion | flops 1222901760 | bytes 7120896 | tf_op jit(solution)/shard_map/while/body/eval_jaxpr/dot_general | solution.py:39
  206.2 5.2 %all-to-all-start = ((bf16[8,32,1536]{2,1,0:T(8,128)(2,1)}), bf16[8,32,1536]{2,1,0:T(8,128)(2,1)S(1)}, u32[]{:S(2)}, u32[]{:S(2)}) async-start(bf16[8,32,1536]{2,1,0:T(8,128)(2,1)} %all_to_all.18), calls=%async_computation | async-start | bytes 1572864 | tf_op jit(solution)/shard_map/while/body/eval_jaxpr/all_to_all | solution.py:80
  212.7 7.8 %all-to-all-done = bf16[8,32,1536]{2,1,0:T(8,128)(2,1)S(1)} async-done(((bf16[8,32,1536]{2,1,0:T(8,128)(2,1)}), bf16[8,32,1536]{2,1,0:T(8,128)(2,1)S(1)}, u32[]{:S(2)}, u32[]{:S(2)}) %all-to-all-start) | async-done | bytes 786464 | tf_op jit(solution)/shard_map/while/body/eval_jaxpr/all_to_all | solution.py:80
  222.7 9.9 %collective-permute-done.2 = bf16[256,1536]{1,0:T(8,128)(2,1)S(1)} collective-permute-done((bf16[256,1536]{1,0:T(8,128)(2,1)}, bf16[256,1536]{1,0:T(8,128)(2,1)S(1)}, u32[]{:S(2)}, u32[]{:S(2)}) %collective-permute-start.2) | collective-permute-done | bytes 786464 | tf_op jit(solution)/shard_map/while/body/eval_jaxpr/ppermute | solution.py:25
  241.1 5.4 %fusion.52 = bf16[256,1536]{1,0:T(8,128)(2,1)} fusion(bf16[256,1536]{1,0:T(8,128)(2,1)S(1)} %get-tuple-element.323, bf16[1536,1536]{1,0:T(8,128)(2,1)} %get-tuple-element.369, bf16[256,1536]{1,0:T(8,128)(2,1)S(1)} %fusion.50, bf16[2,1536]{1,0:T(2,128)(2,1)S(1)} %collective-permute-done, bf16[2,1536]{1,0:T(2,128)(2,1)S(1)} %collective-permute-done.1, ...), kind=kOutput, calls=%fused_computation.10.clone.1 | convolution fusion | flops 1222901760 | bytes 7120896 | tf_op jit(solution)/shard_map/while/body/eval_jaxpr/dot_general | solution.py:39
  249.6 5.2 %all-to-all-start = ((bf16[8,32,1536]{2,1,0:T(8,128)(2,1)}), bf16[8,32,1536]{2,1,0:T(8,128)(2,1)S(1)}, u32[]{:S(2)}, u32[]{:S(2)}) async-start(bf16[8,32,1536]{2,1,0:T(8,128)(2,1)} %all_to_all.18), calls=%async_computation | async-start | bytes 1572864 | tf_op jit(solution)/shard_map/while/body/eval_jaxpr/all_to_all | solution.py:80
  256.1 7.8 %all-to-all-done = bf16[8,32,1536]{2,1,0:T(8,128)(2,1)S(1)} async-done(((bf16[8,32,1536]{2,1,0:T(8,128)(2,1)}), bf16[8,32,1536]{2,1,0:T(8,128)(2,1)S(1)}, u32[]{:S(2)}, u32[]{:S(2)}) %all-to-all-start) | async-done | bytes 786464 | tf_op jit(solution)/shard_map/while/body/eval_jaxpr/all_to_all | solution.py:80
  266.2 9.9 %collective-permute-done.2 = bf16[256,1536]{1,0:T(8,128)(2,1)S(1)} collective-permute-done((bf16[256,1536]{1,0:T(8,128)(2,1)}, bf16[256,1536]{1,0:T(8,128)(2,1)S(1)}, u32[]{:S(2)}, u32[]{:S(2)}) %collective-permute-start.2) | collective-permute-done | bytes 786464 | tf_op jit(solution)/shard_map/while/body/eval_jaxpr/ppermute | solution.py:25
  284.5 5.4 %fusion.52 = bf16[256,1536]{1,0:T(8,128)(2,1)} fusion(bf16[256,1536]{1,0:T(8,128)(2,1)S(1)} %get-tuple-element.323, bf16[1536,1536]{1,0:T(8,128)(2,1)} %get-tuple-element.369, bf16[256,1536]{1,0:T(8,128)(2,1)S(1)} %fusion.50, bf16[2,1536]{1,0:T(2,128)(2,1)S(1)} %collective-permute-done, bf16[2,1536]{1,0:T(2,128)(2,1)S(1)} %collective-permute-done.1, ...), kind=kOutput, calls=%fused_computation.10.clone.1 | convolution fusion | flops 1222901760 | bytes 7120896 | tf_op jit(solution)/shard_map/while/body/eval_jaxpr/dot_general | solution.py:39
  293.0 5.2 %all-to-all-start = ((bf16[8,32,1536]{2,1,0:T(8,128)(2,1)}), bf16[8,32,1536]{2,1,0:T(8,128)(2,1)S(1)}, u32[]{:S(2)}, u32[]{:S(2)}) async-start(bf16[8,32,1536]{2,1,0:T(8,128)(2,1)} %all_to_all.18), calls=%async_computation | async-start | bytes 1572864 | tf_op jit(solution)/shard_map/while/body/eval_jaxpr/all_to_all | solution.py:80
  299.6 7.8 %all-to-all-done = bf16[8,32,1536]{2,1,0:T(8,128)(2,1)S(1)} async-done(((bf16[8,32,1536]{2,1,0:T(8,128)(2,1)}), bf16[8,32,1536]{2,1,0:T(8,128)(2,1)S(1)}, u32[]{:S(2)}, u32[]{:S(2)}) %all-to-all-start) | async-done | bytes 786464 | tf_op jit(solution)/shard_map/while/body/eval_jaxpr/all_to_all | solution.py:80
  309.6 9.9 %collective-permute-done.2 = bf16[256,1536]{1,0:T(8,128)(2,1)S(1)} collective-permute-done((bf16[256,1536]{1,0:T(8,128)(2,1)}, bf16[256,1536]{1,0:T(8,128)(2,1)S(1)}, u32[]{:S(2)}, u32[]{:S(2)}) %collective-permute-start.2) | collective-permute-done | bytes 786464 | tf_op jit(solution)/shard_map/while/body/eval_jaxpr/ppermute | solution.py:25
  (117 shorter events, 108.0 us)
Async XLA Ops:
  0.0 8.2 %copy-start = (bf16[512,1536]{1,0:T(8,128)(2,1)S(1)}, bf16[512,1536]{1,0:T(8,128)(2,1)}, u32[]{:S(2)}) copy-start(bf16[512,1536]{1,0:T(8,128)(2,1)} %param.9) | copy-start | bytes 4718596
  13.4 1.9 copy-start.1
  17.1 5.7 %collective-permute-start = (bf16[2,1536]{1,0:T(2,128)(2,1)S(1)}, bf16[2,1536]{1,0:T(2,128)(2,1)S(1)}, u32[]{:S(2)}, u32[]{:S(2)}) collective-permute-start(bf16[2,1536]{1,0:T(2,128)(2,1)S(1)} %get-tuple-element.325), channel_id=1, source_target_pairs={{1,0},{2,1},{3,2},{4,3},{5,4},{6,5},{7,6},{9,8},{10,9},{11,10},{12... | collective-permute-start | bytes 18440 | tf_op jit(solution)/shard_map/while/body/eval_jaxpr/ppermute | solution.py:17
  19.7 3.8 %collective-permute-start.1 = (bf16[2,1536]{1,0:T(2,128)(2,1)S(1)}, bf16[2,1536]{1,0:T(2,128)(2,1)S(1)}, u32[]{:S(2)}, u32[]{:S(2)}) collective-permute-start(bf16[2,1536]{1,0:T(2,128)(2,1)S(1)} %get-tuple-element.326), channel_id=1, source_target_pairs={{0,1},{1,2},{2,3},{3,4},{4,5},{5,6},{6,7},{8,9},{9,10},{10,11},{11... | collective-permute-start | bytes 18440 | tf_op jit(solution)/shard_map/while/body/eval_jaxpr/ppermute | solution.py:14
  32.0 14.9 %all-to-all-start = ((bf16[8,32,1536]{2,1,0:T(8,128)(2,1)}), bf16[8,32,1536]{2,1,0:T(8,128)(2,1)S(1)}, u32[]{:S(2)}, u32[]{:S(2)}) async-start(bf16[8,32,1536]{2,1,0:T(8,128)(2,1)} %all_to_all.18), calls=%async_computation | async-start | bytes 1572864 | tf_op jit(solution)/shard_map/while/body/eval_jaxpr/all_to_all | solution.py:80
  37.7 21.3 %collective-permute-start.2 = (bf16[256,1536]{1,0:T(8,128)(2,1)}, bf16[256,1536]{1,0:T(8,128)(2,1)S(1)}, u32[]{:S(2)}, u32[]{:S(2)}) collective-permute-start(bf16[256,1536]{1,0:T(8,128)(2,1)} %fusion.52), channel_id=1, source_target_pairs={{0,8},{8,16},{16,24},{1,9},{9,17},{17,25},{2,10},{10,18},{18,26},{... | collective-permute-start | bytes 2359304 | tf_op jit(solution)/shard_map/while/body/eval_jaxpr/ppermute | solution.py:25
  60.8 6.0 %collective-permute-start = (bf16[2,1536]{1,0:T(2,128)(2,1)S(1)}, bf16[2,1536]{1,0:T(2,128)(2,1)S(1)}, u32[]{:S(2)}, u32[]{:S(2)}) collective-permute-start(bf16[2,1536]{1,0:T(2,128)(2,1)S(1)} %get-tuple-element.325), channel_id=1, source_target_pairs={{1,0},{2,1},{3,2},{4,3},{5,4},{6,5},{7,6},{9,8},{10,9},{11,10},{12... | collective-permute-start | bytes 18440 | tf_op jit(solution)/shard_map/while/body/eval_jaxpr/ppermute | solution.py:17
  63.5 4.0 %collective-permute-start.1 = (bf16[2,1536]{1,0:T(2,128)(2,1)S(1)}, bf16[2,1536]{1,0:T(2,128)(2,1)S(1)}, u32[]{:S(2)}, u32[]{:S(2)}) collective-permute-start(bf16[2,1536]{1,0:T(2,128)(2,1)S(1)} %get-tuple-element.326), channel_id=1, source_target_pairs={{0,1},{1,2},{2,3},{3,4},{4,5},{5,6},{6,7},{8,9},{9,10},{10,11},{11... | collective-permute-start | bytes 18440 | tf_op jit(solution)/shard_map/while/body/eval_jaxpr/ppermute | solution.py:14
  75.9 14.4 %all-to-all-start = ((bf16[8,32,1536]{2,1,0:T(8,128)(2,1)}), bf16[8,32,1536]{2,1,0:T(8,128)(2,1)S(1)}, u32[]{:S(2)}, u32[]{:S(2)}) async-start(bf16[8,32,1536]{2,1,0:T(8,128)(2,1)} %all_to_all.18), calls=%async_computation | async-start | bytes 1572864 | tf_op jit(solution)/shard_map/while/body/eval_jaxpr/all_to_all | solution.py:80
  81.1 21.3 %collective-permute-start.2 = (bf16[256,1536]{1,0:T(8,128)(2,1)}, bf16[256,1536]{1,0:T(8,128)(2,1)S(1)}, u32[]{:S(2)}, u32[]{:S(2)}) collective-permute-start(bf16[256,1536]{1,0:T(8,128)(2,1)} %fusion.52), channel_id=1, source_target_pairs={{0,8},{8,16},{16,24},{1,9},{9,17},{17,25},{2,10},{10,18},{18,26},{... | collective-permute-start | bytes 2359304 | tf_op jit(solution)/shard_map/while/body/eval_jaxpr/ppermute | solution.py:25
  104.2 6.0 %collective-permute-start = (bf16[2,1536]{1,0:T(2,128)(2,1)S(1)}, bf16[2,1536]{1,0:T(2,128)(2,1)S(1)}, u32[]{:S(2)}, u32[]{:S(2)}) collective-permute-start(bf16[2,1536]{1,0:T(2,128)(2,1)S(1)} %get-tuple-element.325), channel_id=1, source_target_pairs={{1,0},{2,1},{3,2},{4,3},{5,4},{6,5},{7,6},{9,8},{10,9},{11,10},{12... | collective-permute-start | bytes 18440 | tf_op jit(solution)/shard_map/while/body/eval_jaxpr/ppermute | solution.py:17
  106.9 4.0 %collective-permute-start.1 = (bf16[2,1536]{1,0:T(2,128)(2,1)S(1)}, bf16[2,1536]{1,0:T(2,128)(2,1)S(1)}, u32[]{:S(2)}, u32[]{:S(2)}) collective-permute-start(bf16[2,1536]{1,0:T(2,128)(2,1)S(1)} %get-tuple-element.326), channel_id=1, source_target_pairs={{0,1},{1,2},{2,3},{3,4},{4,5},{5,6},{6,7},{8,9},{9,10},{10,11},{11... | collective-permute-start | bytes 18440 | tf_op jit(solution)/shard_map/while/body/eval_jaxpr/ppermute | solution.py:14
  119.3 14.4 %all-to-all-start = ((bf16[8,32,1536]{2,1,0:T(8,128)(2,1)}), bf16[8,32,1536]{2,1,0:T(8,128)(2,1)S(1)}, u32[]{:S(2)}, u32[]{:S(2)}) async-start(bf16[8,32,1536]{2,1,0:T(8,128)(2,1)} %all_to_all.18), calls=%async_computation | async-start | bytes 1572864 | tf_op jit(solution)/shard_map/while/body/eval_jaxpr/all_to_all | solution.py:80
  124.6 21.3 %collective-permute-start.2 = (bf16[256,1536]{1,0:T(8,128)(2,1)}, bf16[256,1536]{1,0:T(8,128)(2,1)S(1)}, u32[]{:S(2)}, u32[]{:S(2)}) collective-permute-start(bf16[256,1536]{1,0:T(8,128)(2,1)} %fusion.52), channel_id=1, source_target_pairs={{0,8},{8,16},{16,24},{1,9},{9,17},{17,25},{2,10},{10,18},{18,26},{... | collective-permute-start | bytes 2359304 | tf_op jit(solution)/shard_map/while/body/eval_jaxpr/ppermute | solution.py:25
  147.6 6.0 %collective-permute-start = (bf16[2,1536]{1,0:T(2,128)(2,1)S(1)}, bf16[2,1536]{1,0:T(2,128)(2,1)S(1)}, u32[]{:S(2)}, u32[]{:S(2)}) collective-permute-start(bf16[2,1536]{1,0:T(2,128)(2,1)S(1)} %get-tuple-element.325), channel_id=1, source_target_pairs={{1,0},{2,1},{3,2},{4,3},{5,4},{6,5},{7,6},{9,8},{10,9},{11,10},{12... | collective-permute-start | bytes 18440 | tf_op jit(solution)/shard_map/while/body/eval_jaxpr/ppermute | solution.py:17
  150.3 4.0 %collective-permute-start.1 = (bf16[2,1536]{1,0:T(2,128)(2,1)S(1)}, bf16[2,1536]{1,0:T(2,128)(2,1)S(1)}, u32[]{:S(2)}, u32[]{:S(2)}) collective-permute-start(bf16[2,1536]{1,0:T(2,128)(2,1)S(1)} %get-tuple-element.326), channel_id=1, source_target_pairs={{0,1},{1,2},{2,3},{3,4},{4,5},{5,6},{6,7},{8,9},{9,10},{10,11},{11... | collective-permute-start | bytes 18440 | tf_op jit(solution)/shard_map/while/body/eval_jaxpr/ppermute | solution.py:14
  162.7 14.4 %all-to-all-start = ((bf16[8,32,1536]{2,1,0:T(8,128)(2,1)}), bf16[8,32,1536]{2,1,0:T(8,128)(2,1)S(1)}, u32[]{:S(2)}, u32[]{:S(2)}) async-start(bf16[8,32,1536]{2,1,0:T(8,128)(2,1)} %all_to_all.18), calls=%async_computation | async-start | bytes 1572864 | tf_op jit(solution)/shard_map/while/body/eval_jaxpr/all_to_all | solution.py:80
  168.0 21.3 %collective-permute-start.2 = (bf16[256,1536]{1,0:T(8,128)(2,1)}, bf16[256,1536]{1,0:T(8,128)(2,1)S(1)}, u32[]{:S(2)}, u32[]{:S(2)}) collective-permute-start(bf16[256,1536]{1,0:T(8,128)(2,1)} %fusion.52), channel_id=1, source_target_pairs={{0,8},{8,16},{16,24},{1,9},{9,17},{17,25},{2,10},{10,18},{18,26},{... | collective-permute-start | bytes 2359304 | tf_op jit(solution)/shard_map/while/body/eval_jaxpr/ppermute | solution.py:25
  191.1 6.0 %collective-permute-start = (bf16[2,1536]{1,0:T(2,128)(2,1)S(1)}, bf16[2,1536]{1,0:T(2,128)(2,1)S(1)}, u32[]{:S(2)}, u32[]{:S(2)}) collective-permute-start(bf16[2,1536]{1,0:T(2,128)(2,1)S(1)} %get-tuple-element.325), channel_id=1, source_target_pairs={{1,0},{2,1},{3,2},{4,3},{5,4},{6,5},{7,6},{9,8},{10,9},{11,10},{12... | collective-permute-start | bytes 18440 | tf_op jit(solution)/shard_map/while/body/eval_jaxpr/ppermute | solution.py:17
  193.8 4.0 %collective-permute-start.1 = (bf16[2,1536]{1,0:T(2,128)(2,1)S(1)}, bf16[2,1536]{1,0:T(2,128)(2,1)S(1)}, u32[]{:S(2)}, u32[]{:S(2)}) collective-permute-start(bf16[2,1536]{1,0:T(2,128)(2,1)S(1)} %get-tuple-element.326), channel_id=1, source_target_pairs={{0,1},{1,2},{2,3},{3,4},{4,5},{5,6},{6,7},{8,9},{9,10},{10,11},{11... | collective-permute-start | bytes 18440 | tf_op jit(solution)/shard_map/while/body/eval_jaxpr/ppermute | solution.py:14
  206.2 14.4 %all-to-all-start = ((bf16[8,32,1536]{2,1,0:T(8,128)(2,1)}), bf16[8,32,1536]{2,1,0:T(8,128)(2,1)S(1)}, u32[]{:S(2)}, u32[]{:S(2)}) async-start(bf16[8,32,1536]{2,1,0:T(8,128)(2,1)} %all_to_all.18), calls=%async_computation | async-start | bytes 1572864 | tf_op jit(solution)/shard_map/while/body/eval_jaxpr/all_to_all | solution.py:80
  211.4 21.3 %collective-permute-start.2 = (bf16[256,1536]{1,0:T(8,128)(2,1)}, bf16[256,1536]{1,0:T(8,128)(2,1)S(1)}, u32[]{:S(2)}, u32[]{:S(2)}) collective-permute-start(bf16[256,1536]{1,0:T(8,128)(2,1)} %fusion.52), channel_id=1, source_target_pairs={{0,8},{8,16},{16,24},{1,9},{9,17},{17,25},{2,10},{10,18},{18,26},{... | collective-permute-start | bytes 2359304 | tf_op jit(solution)/shard_map/while/body/eval_jaxpr/ppermute | solution.py:25
  234.5 6.0 %collective-permute-start = (bf16[2,1536]{1,0:T(2,128)(2,1)S(1)}, bf16[2,1536]{1,0:T(2,128)(2,1)S(1)}, u32[]{:S(2)}, u32[]{:S(2)}) collective-permute-start(bf16[2,1536]{1,0:T(2,128)(2,1)S(1)} %get-tuple-element.325), channel_id=1, source_target_pairs={{1,0},{2,1},{3,2},{4,3},{5,4},{6,5},{7,6},{9,8},{10,9},{11,10},{12... | collective-permute-start | bytes 18440 | tf_op jit(solution)/shard_map/while/body/eval_jaxpr/ppermute | solution.py:17
  237.2 4.0 %collective-permute-start.1 = (bf16[2,1536]{1,0:T(2,128)(2,1)S(1)}, bf16[2,1536]{1,0:T(2,128)(2,1)S(1)}, u32[]{:S(2)}, u32[]{:S(2)}) collective-permute-start(bf16[2,1536]{1,0:T(2,128)(2,1)S(1)} %get-tuple-element.326), channel_id=1, source_target_pairs={{0,1},{1,2},{2,3},{3,4},{4,5},{5,6},{6,7},{8,9},{9,10},{10,11},{11... | collective-permute-start | bytes 18440 | tf_op jit(solution)/shard_map/while/body/eval_jaxpr/ppermute | solution.py:14
  249.6 14.4 %all-to-all-start = ((bf16[8,32,1536]{2,1,0:T(8,128)(2,1)}), bf16[8,32,1536]{2,1,0:T(8,128)(2,1)S(1)}, u32[]{:S(2)}, u32[]{:S(2)}) async-start(bf16[8,32,1536]{2,1,0:T(8,128)(2,1)} %all_to_all.18), calls=%async_computation | async-start | bytes 1572864 | tf_op jit(solution)/shard_map/while/body/eval_jaxpr/all_to_all | solution.py:80
  254.8 21.3 %collective-permute-start.2 = (bf16[256,1536]{1,0:T(8,128)(2,1)}, bf16[256,1536]{1,0:T(8,128)(2,1)S(1)}, u32[]{:S(2)}, u32[]{:S(2)}) collective-permute-start(bf16[256,1536]{1,0:T(8,128)(2,1)} %fusion.52), channel_id=1, source_target_pairs={{0,8},{8,16},{16,24},{1,9},{9,17},{17,25},{2,10},{10,18},{18,26},{... | collective-permute-start | bytes 2359304 | tf_op jit(solution)/shard_map/while/body/eval_jaxpr/ppermute | solution.py:25
  277.9 6.0 %collective-permute-start = (bf16[2,1536]{1,0:T(2,128)(2,1)S(1)}, bf16[2,1536]{1,0:T(2,128)(2,1)S(1)}, u32[]{:S(2)}, u32[]{:S(2)}) collective-permute-start(bf16[2,1536]{1,0:T(2,128)(2,1)S(1)} %get-tuple-element.325), channel_id=1, source_target_pairs={{1,0},{2,1},{3,2},{4,3},{5,4},{6,5},{7,6},{9,8},{10,9},{11,10},{12... | collective-permute-start | bytes 18440 | tf_op jit(solution)/shard_map/while/body/eval_jaxpr/ppermute | solution.py:17
  280.6 4.0 %collective-permute-start.1 = (bf16[2,1536]{1,0:T(2,128)(2,1)S(1)}, bf16[2,1536]{1,0:T(2,128)(2,1)S(1)}, u32[]{:S(2)}, u32[]{:S(2)}) collective-permute-start(bf16[2,1536]{1,0:T(2,128)(2,1)S(1)} %get-tuple-element.326), channel_id=1, source_target_pairs={{0,1},{1,2},{2,3},{3,4},{4,5},{5,6},{6,7},{8,9},{9,10},{10,11},{11... | collective-permute-start | bytes 18440 | tf_op jit(solution)/shard_map/while/body/eval_jaxpr/ppermute | solution.py:14
  293.0 14.4 %all-to-all-start = ((bf16[8,32,1536]{2,1,0:T(8,128)(2,1)}), bf16[8,32,1536]{2,1,0:T(8,128)(2,1)S(1)}, u32[]{:S(2)}, u32[]{:S(2)}) async-start(bf16[8,32,1536]{2,1,0:T(8,128)(2,1)} %all_to_all.18), calls=%async_computation | async-start | bytes 1572864 | tf_op jit(solution)/shard_map/while/body/eval_jaxpr/all_to_all | solution.py:80
  298.3 21.3 %collective-permute-start.2 = (bf16[256,1536]{1,0:T(8,128)(2,1)}, bf16[256,1536]{1,0:T(8,128)(2,1)S(1)}, u32[]{:S(2)}, u32[]{:S(2)}) collective-permute-start(bf16[256,1536]{1,0:T(8,128)(2,1)} %fusion.52), channel_id=1, source_target_pairs={{0,8},{8,16},{16,24},{1,9},{9,17},{17,25},{2,10},{10,18},{18,26},{... | collective-permute-start | bytes 2359304 | tf_op jit(solution)/shard_map/while/body/eval_jaxpr/ppermute | solution.py:25
where the time goes:
time: 322 us; the launch traced here: 320 us
  waiting for transfers between devices  129 us (40%)
  starting transfers between devices  87 us (27%)
  matrix products  45.4 us (14%)
  local copies, waits for them, and re-layouts  29 us (9%)
  other arithmetic  28.6 us (9%)
    ppermute x7, waiting for transfers between devices, passed_along(): lax.ppermute(value, axis, [(source, source + steps) for source in range(i...  69.5 us
    all_to_all x7, waiting for transfers between devices, advance(): lax.all_to_all(arrange(leaving), 'seq', split_axis=0, concat_axis=0, tile...  54.8 us
    dot_general x7, matrix products, section_block(): update = jnp.dot(mixed, weight, preferred_element_type=jnp.float32)  37.8 us
    all_to_all x7, starting transfers between devices, advance(): lax.all_to_all(arrange(leaving), 'seq', split_axis=0, concat_axis=0, tile...  37.1 us
    ppermute x7, starting transfers between devices, extended(): lax.ppermute(lax.slice_in_dim(block, block.shape[dim] - width, None, axis...  22.2 us
    ppermute x7, starting transfers between devices, extended(): lax.ppermute(lax.slice_in_dim(block, 0, width, axis=dim), axis, backward)  18.7 us
    dynamic_update_slice x7, other arithmetic, advance(): hint_rows = lax.dynamic_update_index_in_dim(hint_rows, arrived, slot_idx, 0)  15.4 us
    reduce_sum x7, other arithmetic, section_block(): jnp.mean(wide_state * wide_state, axis=-1, keepdims=True) + 1e-06  10.4 us
  transfers between devices with their start and end apart: 28, of which 21 were waited for; matrix products, arithmetic and copies ran while one was open for 5% of the time, Pallas kernels for 0%

commit v1 on v0

v1 whole, which is shorter than its diff:
```python
import functools

import jax
import jax.numpy as jnp
from jax import lax
from jax.experimental import pallas as pl
from jax.experimental.pallas import tpu as pltpu
from jax.sharding import PartitionSpec as P

BLOCK_BP = 128
CHUNK = 64
LEAD = 8
MESH = pl.DeviceIdType.MESH


def kernel(
    sizes,
    bases_ref,
    stem_ref,
    gain_ref,
    taps_ref,
    weight_ref,
    order_ref,
    out_ref,
    codes,
    arriving,
    leaving,
    ordered,
    state_buf,
    normed_buf,
    mixed_buf,
    codes_send,
    codes_recv,
    local_sem,
    state_send,
    state_recv,
    hint_send,
    hint_recv,
    own_sem,
):
    micro, rows, halo, sections, peers, reach = sizes
    channels = weight_ref.shape[1]
    span = rows + 2 * halo
    chunks = micro * span // CHUNK
    share = rows // peers
    taps = 2 * reach + 1
    sec = lax.axis_index("section")
    me = lax.axis_index("seq")
    first, last = sec == 0, sec == sections - 1
    col_tile = 256
    out_tile = 512

    barrier = pltpu.get_barrier_semaphore()

    def greet(k, carry):
        pl.semaphore_signal(
            barrier, inc=1, device_id={"seq": lax.rem(me + k, peers)}, device_id_type=MESH
        )
        return carry

    lax.fori_loop(1, peers, greet, 0)

    @pl.when(sec > 0)
    def _():
        pl.semaphore_signal(barrier, inc=1, device_id={"section": sec - 1}, device_id_type=MESH)

    @pl.when(last)
    def _():
        pl.semaphore_wait(barrier, peers - 1)

    @pl.when(jnp.logical_not(last))
    def _():
        pl.semaphore_wait(barrier, peers)

    state_buf[0:LEAD] = jnp.zeros((LEAD, channels), jnp.float32)
    normed_buf[0:LEAD] = jnp.zeros((LEAD, channels), jnp.float32)

    def to_right(m):
        return pltpu.make_async_remote_copy(
            src_ref=bases_ref.at[m, pl.ds(rows - halo, halo)],
            dst_ref=codes.at[pl.ds(m * span, halo)],
            send_sem=codes_send.at[0, m],
            recv_sem=codes_recv.at[0, m],
            device_id={"seq": me + 1},
            device_id_type=MESH,
        )

    def to_left(m):
        return pltpu.make_async_remote_copy(
            src_ref=bases_ref.at[m, pl.ds(0, halo)],
            dst_ref=codes.at[pl.ds(m * span + halo + rows, halo)],
            send_sem=codes_send.at[1, m],
            recv_sem=codes_recv.at[1, m],
            device_id={"seq": me - 1},
            device_id_type=MESH,
        )

    @pl.when(first)
    def _():
        @pl.when(me < peers - 1)
        def _():
            for m in range(micro):
                to_right(m).start()

        @pl.when(me > 0)
        def _():
            for m in range(micro):
                to_left(m).start()

        for m in range(micro):
            codes[m * span + halo : m * span + halo + rows] = bases_ref[m]

        @pl.when(me == 0)
        def _():
            for m in range(micro):
                codes[m * span : m * span + halo] = jnp.zeros((halo, BLOCK_BP), jnp.int32)

        @pl.when(me == peers - 1)
        def _():
            for m in range(micro):
                low = m * span + halo + rows
                codes[low : low + halo] = jnp.zeros((halo, BLOCK_BP), jnp.int32)

        @pl.when(me < peers - 1)
        def _():
            for m in range(micro):
                to_right(m).wait_send()
                to_left(m).wait_recv()

        @pl.when(me > 0)
        def _():
            for m in range(micro):
                to_left(m).wait_send()
                to_right(m).wait_recv()

    def state_copy(i):
        part = pl.ds(pl.multiple_of(i * CHUNK, CHUNK), CHUNK)
        return pltpu.make_async_remote_copy(
            src_ref=leaving.at[part],
            dst_ref=arriving.at[part],
            send_sem=state_send.at[i],
            recv_sem=state_recv.at[i],
            device_id={"section": sec + 1},
            device_id_type=MESH,
        )

    def hint_copy(m, k):
        peer = lax.rem(me + k, peers)
        return pltpu.make_async_remote_copy(
            src_ref=ordered.at[m, peer],
            dst_ref=out_ref.at[m, me],
            send_sem=hint_send.at[m, k - 1],
            recv_sem=hint_recv.at[m, k - 1],
            device_id={"seq": peer},
            device_id_type=MESH,
        )

    def own_copy(m):
        return pltpu.make_async_copy(ordered.at[m, me], out_ref.at[m, me], own_sem.at[m])

    def step(i, carry):
        base = pl.multiple_of(i * CHUNK, CHUNK)
        state_buf[0:LEAD] = state_buf[CHUNK : CHUNK + LEAD]
        normed_buf[0:LEAD] = normed_buf[CHUNK : CHUNK + LEAD]

        @pl.when(first)
        def _():
            code = codes[pl.ds(base, CHUNK)].astype(jnp.bfloat16)
            wide = 4 * BLOCK_BP
            spread = (
                lax.broadcasted_iota(jnp.int32, (BLOCK_BP, wide), 1) // 4
                == lax.broadcasted_iota(jnp.int32, (BLOCK_BP, wide), 0)
            )
            spread = jnp.where(spread, 1.0, 0.0).astype(jnp.bfloat16)
            repeated = jnp.dot(code, spread, preferred_element_type=jnp.float32)
            letter = lax.broadcasted_iota(jnp.int32, (CHUNK, wide), 1) % 4
            onehot = jnp.where(repeated == letter.astype(jnp.float32), 1.0, 0.0)
            onehot = onehot.astype(jnp.bfloat16)
            for c in range(0, channels, out_tile):
                part = jnp.dot(
                    onehot, stem_ref[:, c : c + out_tile], preferred_element_type=jnp.float32
                )
                state_buf[LEAD : LEAD + CHUNK, c : c + out_tile] = part.astype(
                    jnp.bfloat16
                ).astype(jnp.float32)

        @pl.when(jnp.logical_not(first))
        def _():
            state_copy(i).wait_recv()
            for c in range(0, channels, col_tile):
                state_buf[LEAD : LEAD + CHUNK, c : c + col_tile] = arriving[
                    pl.ds(base, CHUNK), c : c + col_tile
                ].astype(jnp.float32)

        total = jnp.zeros((CHUNK, 128), jnp.float32)
        for c in range(0, channels, 128):
            part = state_buf[LEAD : LEAD + CHUNK, c : c + 128]
            total = total + part * part
        mean = jnp.sum(total, axis=-1, keepdims=True) * (1.0 / channels)
        inv_rms = lax.rsqrt(mean + 1e-06)
        place = lax.broadcasted_iota(jnp.int32, (CHUNK, 1), 0) + (base - reach * sec)
        low_end = (place >= 0) & (place < halo)
        high_end = (place >= span - halo) & (place < span)
        for m in range(1, micro):
            at = m * span
            low_end = low_end | ((place >= at) & (place < at + halo))
            high_end = high_end | ((place >= at + span - halo) & (place < at + span))
        outside = (low_end & (me == 0)) | (high_end & (me == peers - 1))
        inv_rms = jnp.where(outside, 0.0, inv_rms)

        for c in range(0, channels, col_tile):
            cols = slice(c, c + col_tile)
            normed = state_buf[LEAD : LEAD + CHUNK, cols] * inv_rms * gain_ref[:, cols]
            normed_buf[LEAD : LEAD + CHUNK, cols] = normed.astype(jnp.bfloat16).astype(jnp.float32)
            mixed = jnp.zeros((CHUNK, col_tile), jnp.float32)
            for k in range(taps):
                low = LEAD - 2 * reach + k
                mixed = mixed + taps_ref[0, k : k + 1, cols] * normed_buf[low : low + CHUNK, cols]
            mixed_buf[:, cols] = mixed.astype(jnp.bfloat16)

        for c in range(0, channels, out_tile):
            cols = slice(c, c + out_tile)
            update = jnp.dot(
                mixed_buf[...], weight_ref[0, :, cols], preferred_element_type=jnp.float32
            )
            low = LEAD - reach
            result = state_buf[low : low + CHUNK, cols] + jax.nn.gelu(update)
            leaving[pl.ds(base, CHUNK), cols] = result.astype(jnp.bfloat16)

        @pl.when(jnp.logical_not(last))
        def _():
            state_copy(i).start()

        m = (i * CHUNK) // span

        @pl.when(((i + 1) * CHUNK) // span > m)
        def _():
            top = pl.multiple_of(m * span, 16)
            for c in range(0, channels, out_tile):
                cols = slice(c, c + out_tile)
                moved = jnp.dot(
                    order_ref[...],
                    leaving[pl.ds(top, span), cols],
                    preferred_element_type=jnp.float32,
                )
                ordered[m, :, :, cols] = moved.astype(jnp.bfloat16).reshape(
                    peers, share, out_tile
                )

            def send(k, carry):
                hint_copy(m, k).start()
                return carry

            lax.fori_loop(1, peers, send, 0)
            own_copy(m).start()

        return carry

    lax.fori_loop(0, chunks, step, 0)

    @pl.when(jnp.logical_not(last))
    def _():
        def drain(i, carry):
            state_copy(i).wait_send()
            return carry

        lax.fori_loop(0, chunks, drain, 0)

    for m in range(micro):
        def finish(k, carry):
            copy = hint_copy(m, k)
            copy.wait_send()
            copy.wait_recv()
            return carry

        lax.fori_loop(1, peers, finish, 0)
        own_copy(m).wait()


def on_device(bases, stem_weight, norm_gain, conv_taps, proj_weight, dest):
    micro = bases.shape[0]
    rows = bases.shape[1] // BLOCK_BP
    channels = stem_weight.shape[1]
    sections = lax.axis_size("section")
    peers = lax.axis_size("seq")
    segs_dev = dest.shape[0]
    per_peer = segs_dev // peers
    seg_rows = rows // segs_dev
    share = rows // peers
    reach = conv_taps.shape[1] // 2
    halo = reach * sections
    span = rows + 2 * halo
    chunks = micro * span // CHUNK
    assert halo % 8 == 0 and (micro * span) % CHUNK == 0 and CHUNK <= span
    assert 2 * reach <= LEAD

    send_slot = dest // segs_dev * per_peer + dest % segs_dev % per_peer
    place = jnp.arange(seg_rows, dtype=jnp.int32)
    target = (send_slot[:, None] * seg_rows + place[None, :]).reshape(rows)
    lag = halo + reach * (lax.axis_index("section") + 1)
    from_row = jnp.arange(rows, dtype=jnp.int32) + lag
    by_target = target[:, None] == jnp.arange(rows, dtype=jnp.int32)[None, :]
    by_source = from_row[:, None] == jnp.arange(span, dtype=jnp.int32)[None, :]
    order = jnp.dot(
        by_target.astype(jnp.bfloat16).T,
        by_source.astype(jnp.bfloat16),
        preferred_element_type=jnp.float32,
    ).astype(jnp.bfloat16)

    vmem = pl.BlockSpec(memory_space=pltpu.VMEM)
    dma = pltpu.SemaphoreType.DMA
    hints = pl.pallas_call(
        functools.partial(kernel, (micro, rows, halo, sections, peers, reach)),
        out_shape=jax.ShapeDtypeStruct((micro, peers, share, channels), jnp.bfloat16),
        in_specs=[vmem] * 6,
        out_specs=vmem,
        scratch_shapes=[
            pltpu.VMEM((micro * span, BLOCK_BP), jnp.int32),
            pltpu.VMEM((micro * span, channels), jnp.bfloat16),
            pltpu.VMEM((micro * span, channels), jnp.bfloat16),
            pltpu.VMEM((micro, peers, share, channels), jnp.bfloat16),
            pltpu.VMEM((LEAD + CHUNK, channels), jnp.float32),
            pltpu.VMEM((LEAD + CHUNK, channels), jnp.float32),
            pltpu.VMEM((CHUNK, channels), jnp.bfloat16),
            dma((2, micro)),
            dma((2, micro)),
            dma,
            dma((chunks,)),
            dma((chunks,)),
            dma((micro, peers - 1)),
            dma((micro, peers - 1)),
            dma((micro,)),
        ],
        compiler_params=pltpu.CompilerParams(
            collective_id=0, has_side_effects=True, vmem_limit_bytes=48 * 1024 * 1024
        ),
    )(
        bases.reshape(micro, rows, BLOCK_BP),
        stem_weight,
        norm_gain,
        conv_taps,
        proj_weight,
        order,
    )
    return hints.reshape(1, micro, rows, channels)


def solution(mesh):
    return jax.shard_map(
        on_device,
        mesh=mesh,
        in_specs=(
            P(None, "seq"),
            P(),
            P("section", None),
            P("section", None, None),
            P("section", None, None),
            P("seq"),
        ),
        out_specs=P("section", None, "seq", None),
        check_vma=False,
    )
```

time: 322 us -> 114 us (0.35)
  waiting for transfers between devices: 129 us -> 0 us
  Pallas kernels: 0 us -> 106 us
  starting transfers between devices: 87 us -> 0 us
  matrix products: 45.4 us -> 0.34 us
  other arithmetic: 28.6 us -> 0.75 us
  local copies, waits for them, and re-layouts: 29 us -> 5.86 us
    pallas_call x0 -> x1, Pallas kernels: none -> 106 us  [on_device(): pl.pallas_call(functools.partial(kernel, (micro, rows, halo, sections, pe...]
    ppermute x21 -> x0, waiting for transfers between devices: 74.1 us -> none  [the longest x7 69.5 us: passed_along(): lax.ppermute(value, axis, [(source, source + steps) for source in range(i...]
    all_to_all x7 -> x0, waiting for transfers between devices: 54.8 us -> none  [advance(): lax.all_to_all(arrange(leaving), 'seq', split_axis=0, concat_axis=0, tile...]
    ppermute x21 -> x0, starting transfers between devices: 49.9 us -> none  [the longest x7 22.2 us: extended(): lax.ppermute(lax.slice_in_dim(block, block.shape[dim] - width, None, axis...]
    dot_general x15 -> x1, matrix products: 45.4 us -> 0.34 us  [on_device(): jnp.dot(by_target.astype(jnp.bfloat16).T, by_source.astype(jnp.bfloat16),...]
    all_to_all x7 -> x0, starting transfers between devices: 37.1 us -> none  [advance(): lax.all_to_all(arrange(leaving), 'seq', split_axis=0, concat_axis=0, tile...]
    dynamic_update_slice x7 -> x0, other arithmetic: 15.4 us -> none  [advance(): hint_rows = lax.dynamic_update_index_in_dim(hint_rows, arrived, slot_idx, 0)]
    reduce_sum x7 -> x0, other arithmetic: 10.4 us -> none  [section_block(): jnp.mean(wide_state * wide_state, axis=-1, keepdims=True) + 1e-06]
  transfers between devices with their start and end apart: 28 -> 0, of which waited for: 21 -> 0; matrix products, arithmetic and copies ran while one was open for 5% -> 0% of each run, Pallas kernels for 0% -> 0%
where the time goes in v1:
time: 114 us; the launch traced here: 113 us
  Pallas kernels  106 us (93%)
  local copies, waits for them, and re-layouts  5.86 us (5%)
    pallas_call x1, Pallas kernels, on_device(): pl.pallas_call(functools.partial(kernel, (micro, rows, halo, sections, pe...  106 us
    unnamed x7, local copies, waits for them, and re-layouts  5.6 us

profile of v1, /device:TPU:25, one launch (start us, length us, event | category | flops | bytes accessed | tf_op | source)
XLA Modules:
  0.0 113.4 jit_solution(4252423618086744698)
XLA Ops:
  0.0 0.7 fusion.4
  0.7 0.1 iota_add_fusion
  0.8 0.1 add.56
  0.8 0.8 copy.11.taps_ref
  1.6 0.3 convolution_convert_fusion
  2.0 0.2 copy.12.order_ref
  2.1 1.1 copy.15
  3.2 0.0 copy-start
  3.2 1.4 %copy-done = bf16[512,1536]{1,0:T(8,128)(2,1)S(1)} copy-done((bf16[512,1536]{1,0:T(8,128)(2,1)S(1)}, bf16[512,1536]{1,0:T(8,128)(2,1)}, u32[]{:S(2)}) %copy-start) | copy-done | bytes 1572888
  4.6 0.0 copy-start.1
  4.6 0.7 copy-done.1
  5.3 106.4 %shard_map.64 = bf16[4,8,32,1536]{3,2,1,0:T(8,128)(2,1)S(1)} custom-call(s32[4,256,128]{2,1,0:T(8,128)S(1)} %bitcast.6, bf16[512,1536]{1,0:T(8,128)(2,1)S(1)} %copy-done, f32[1,1536]{1,0:T(1,128)S(1)} %copy-done.1, f32[1,5,1536]{2,1,0:T(8,128)S(1)} %copy.11.taps_ref, bf16[1,1536,1536]{2,1,0:T(8,128)(2,1)} %weight_ref.1, bf16[256,272]{1,0:T(8,128)(2,1)S(1)} %copy.12.order_ref), custom_call_target="tpu_custom_call" | custom-call | tf_op jit(solution)/shard_map/pallas_call | solution.py:312
  111.7 1.7 %copy.17 = bf16[1,4,256,1536]{3,2,1,0:T(8,128)(2,1)} copy(bf16[1,4,256,1536]{3,2,1,0:T(8,128)(2,1)S(1)} %bitcast.5) | data formatting | bytes 6291456
  (1 shorter events, 0.0 us)
Async XLA Ops:
  3.2 1.4 %copy-start = (bf16[512,1536]{1,0:T(8,128)(2,1)S(1)}, bf16[512,1536]{1,0:T(8,128)(2,1)}, u32[]{:S(2)}) copy-start(bf16[512,1536]{1,0:T(8,128)(2,1)} %stem_ref.1) | copy-start | bytes 4718596
  4.6 0.7 copy-start.1

commit v2 on v1

--- a/solution.py
+++ b/solution.py
@@ -8,7 +8,7 @@
 from jax.sharding import PartitionSpec as P
 
 BLOCK_BP = 128
-CHUNK = 64
+CHUNK = 32
 LEAD = 8
 MESH = pl.DeviceIdType.MESH
 
@@ -16,12 +16,17 @@
 def kernel(
     sizes,
     bases_ref,
+    stem_hbm,
+    gain_hbm,
+    taps_hbm,
+    weight_hbm,
+    dest_ref,
+    out_ref,
     stem_ref,
     gain_ref,
     taps_ref,
     weight_ref,
     order_ref,
-    out_ref,
     codes,
     arriving,
     leaving,
@@ -40,6 +45,9 @@
 ):
     micro, rows, halo, sections, peers, reach = sizes
     channels = weight_ref.shape[1]
+    segs_dev = dest_ref.shape[1]
+    per_peer = segs_dev // peers
+    seg_rows = rows // segs_dev
     span = rows + 2 * halo
     chunks = micro * span // CHUNK
     share = rows // peers
@@ -50,6 +58,20 @@
     col_tile = 256
     out_tile = 512
 
+    loads = [
+        pltpu.make_async_copy(src, dst, local_sem.at[n])
+        for n, (src, dst) in enumerate(
+            (
+                (gain_hbm, gain_ref),
+                (taps_hbm, taps_ref),
+                (stem_hbm, stem_ref),
+                (weight_hbm, weight_ref),
+            )
+        )
+    ]
+    for load in loads:
+        load.start()
+
     barrier = pltpu.get_barrier_semaphore()
 
     def greet(k, carry):
@@ -64,6 +86,14 @@
     def _():
         pl.semaphore_signal(barrier, inc=1, device_id={"section": sec - 1}, device_id_type=MESH)
 
+    @pl.when(first)
+    def _():
+        for m in range(micro):
+            codes[m * span + halo : m * span + halo + rows] = bases_ref[:, m, :]
+
+    state_buf[CHUNK : CHUNK + LEAD] = jnp.zeros((LEAD, channels), jnp.float32)
+    normed_buf[CHUNK : CHUNK + LEAD] = jnp.zeros((LEAD, channels), jnp.float32)
+
     @pl.when(last)
     def _():
         pl.semaphore_wait(barrier, peers - 1)
@@ -71,13 +101,10 @@
     @pl.when(jnp.logical_not(last))
     def _():
         pl.semaphore_wait(barrier, peers)
-
-    state_buf[0:LEAD] = jnp.zeros((LEAD, channels), jnp.float32)
-    normed_buf[0:LEAD] = jnp.zeros((LEAD, channels), jnp.float32)
 
     def to_right(m):
         return pltpu.make_async_remote_copy(
-            src_ref=bases_ref.at[m, pl.ds(rows - halo, halo)],
+            src_ref=codes.at[pl.ds(m * span + rows, halo)],
             dst_ref=codes.at[pl.ds(m * span, halo)],
             send_sem=codes_send.at[0, m],
             recv_sem=codes_recv.at[0, m],
@@ -87,7 +114,7 @@
 
     def to_left(m):
         return pltpu.make_async_remote_copy(
-            src_ref=bases_ref.at[m, pl.ds(0, halo)],
+            src_ref=codes.at[pl.ds(m * span + halo, halo)],
             dst_ref=codes.at[pl.ds(m * span + halo + rows, halo)],
             send_sem=codes_send.at[1, m],
             recv_sem=codes_recv.at[1, m],
@@ -107,9 +134,6 @@
             for m in range(micro):
                 to_left(m).start()
 
-        for m in range(micro):
-            codes[m * span + halo : m * span + halo + rows] = bases_ref[m]
-
         @pl.when(me == 0)
         def _():
             for m in range(micro):
@@ -132,6 +156,33 @@
             for m in range(micro):
                 to_left(m).wait_send()
                 to_right(m).wait_recv()
+
+    iota = functools.partial(lax.broadcasted_iota, jnp.int32)
+
+    def zero_one(flags):
+        return jnp.where(flags, 1.0, 0.0).astype(jnp.bfloat16)
+
+    def build_order():
+        dest_row = dest_ref[...]
+        slot = lax.div(dest_row, segs_dev) * per_peer + lax.rem(
+            lax.rem(dest_row, segs_dev), per_peer
+        )
+        runs = zero_one(iota((segs_dev, segs_dev), 0) == slot)
+        by_slot = zero_one(
+            lax.div(iota((rows, segs_dev), 0), seg_rows) == iota((rows, segs_dev), 1)
+        )
+        lag = halo + reach * (sec + 1)
+        source = iota((segs_dev, span), 1) - lag
+        by_run = zero_one(
+            (source >= 0)
+            & (lax.div(jnp.maximum(source, 0), seg_rows) == iota((segs_dev, span), 0))
+        )
+        picked = jnp.dot(by_slot, runs, preferred_element_type=jnp.float32).astype(jnp.bfloat16)
+        picked = jnp.dot(picked, by_run, preferred_element_type=jnp.float32)
+        phase = lax.rem(
+            iota((rows, span), 0) - iota((rows, span), 1) + (lag + seg_rows * span), seg_rows
+        )
+        order_ref[...] = jnp.where(phase == 0, picked, 0.0).astype(jnp.bfloat16)
 
     def state_copy(i):
         part = pl.ds(pl.multiple_of(i * CHUNK, CHUNK), CHUNK)
@@ -215,7 +266,7 @@
             mixed = jnp.zeros((CHUNK, col_tile), jnp.float32)
             for k in range(taps):
                 low = LEAD - 2 * reach + k
-                mixed = mixed + taps_ref[0, k : k + 1, cols] * normed_buf[low : low + CHUNK, cols]
+                mixed = mixed + taps_ref[k, :, cols] * normed_buf[low : low + CHUNK, cols]
             mixed_buf[:, cols] = mixed.astype(jnp.bfloat16)
 
         for c in range(0, channels, out_tile):
@@ -256,6 +307,9 @@
 
         return carry
 
+    build_order()
+    for load in loads:
+        load.wait()
     lax.fori_loop(0, chunks, step, 0)
 
     @pl.when(jnp.logical_not(last))
@@ -284,37 +338,29 @@
     sections = lax.axis_size("section")
     peers = lax.axis_size("seq")
     segs_dev = dest.shape[0]
-    per_peer = segs_dev // peers
-    seg_rows = rows // segs_dev
     share = rows // peers
-    reach = conv_taps.shape[1] // 2
+    taps = conv_taps.shape[1]
+    reach = taps // 2
     halo = reach * sections
     span = rows + 2 * halo
     chunks = micro * span // CHUNK
     assert halo % 8 == 0 and (micro * span) % CHUNK == 0 and CHUNK <= span
     assert 2 * reach <= LEAD
 
-    send_slot = dest // segs_dev * per_peer + dest % segs_dev % per_peer
-    place = jnp.arange(seg_rows, dtype=jnp.int32)
-    target = (send_slot[:, None] * seg_rows + place[None, :]).reshape(rows)
-    lag = halo + reach * (lax.axis_index("section") + 1)
-    from_row = jnp.arange(rows, dtype=jnp.int32) + lag
-    by_target = target[:, None] == jnp.arange(rows, dtype=jnp.int32)[None, :]
-    by_source = from_row[:, None] == jnp.arange(span, dtype=jnp.int32)[None, :]
-    order = jnp.dot(
-        by_target.astype(jnp.bfloat16).T,
-        by_source.astype(jnp.bfloat16),
-        preferred_element_type=jnp.float32,
-    ).astype(jnp.bfloat16)
-
     vmem = pl.BlockSpec(memory_space=pltpu.VMEM)
+    hbm = pl.BlockSpec(memory_space=pl.ANY)
     dma = pltpu.SemaphoreType.DMA
     hints = pl.pallas_call(
         functools.partial(kernel, (micro, rows, halo, sections, peers, reach)),
         out_shape=jax.ShapeDtypeStruct((micro, peers, share, channels), jnp.bfloat16),
-        in_specs=[vmem] * 6,
+        in_specs=[vmem, hbm, hbm, hbm, hbm, vmem],
         out_specs=vmem,
         scratch_shapes=[
+            pltpu.VMEM(stem_weight.shape, stem_weight.dtype),
+            pltpu.VMEM(norm_gain.shape, norm_gain.dtype),
+            pltpu.VMEM((taps, 1, channels), conv_taps.dtype),
+            pltpu.VMEM(proj_weight.shape, proj_weight.dtype),
+            pltpu.VMEM((rows, span), jnp.bfloat16),
             pltpu.VMEM((micro * span, BLOCK_BP), jnp.int32),
             pltpu.VMEM((micro * span, channels), jnp.bfloat16),
             pltpu.VMEM((micro * span, channels), jnp.bfloat16),
@@ -324,7 +370,7 @@
             pltpu.VMEM((CHUNK, channels), jnp.bfloat16),
             dma((2, micro)),
             dma((2, micro)),
-            dma,
+            dma((4,)),
             dma((chunks,)),
             dma((chunks,)),
             dma((micro, peers - 1)),
@@ -332,15 +378,15 @@
             dma((micro,)),
         ],
         compiler_params=pltpu.CompilerParams(
-            collective_id=0, has_side_effects=True, vmem_limit_bytes=48 * 1024 * 1024
+            collective_id=0, has_side_effects=True, vmem_limit_bytes=60 * 1024 * 1024
         ),
     )(
-        bases.reshape(micro, rows, BLOCK_BP),
+        jnp.transpose(bases.reshape(micro, rows, BLOCK_BP), (1, 0, 2)),
         stem_weight,
         norm_gain,
-        conv_taps,
+        jnp.transpose(conv_taps, (1, 0, 2)),
         proj_weight,
-        order,
+        dest.reshape(1, segs_dev),
     )
     return hints.reshape(1, micro, rows, channels)
 

time: 114 us -> 107 us (0.939)
  Pallas kernels: 106 us -> 103 us
  local copies, waits for them, and re-layouts: 5.86 us -> 3.76 us
    pallas_call x1, Pallas kernels: 106 us -> 103 us  [on_device(): pl.pallas_call(functools.partial(kernel, (micro, rows, halo, sections, pe...]
    unnamed x7 -> x1, local copies, waits for them, and re-layouts: 5.6 us -> 3.76 us
where the time goes in v2:
time: 107 us
  Pallas kernels  103 us (96%)
  local copies, waits for them, and re-layouts  3.76 us (4%)
    pallas_call x1, Pallas kernels, on_device(): pl.pallas_call(functools.partial(kernel, (micro, rows, halo, sections, pe...  103 us
    unnamed x1, local copies, waits for them, and re-layouts  3.76 us

profile of v2, /device:TPU:25, one launch (start us, length us, event | category | flops | bytes accessed | tf_op | source)
XLA Modules:
  0.0 107.0 jit_solution(17758635444474753750)
XLA Ops:
  0.0 103.3 %shard_map.64 = bf16[4,8,32,1536]{3,2,1,0:T(8,128)(2,1)} custom-call(s32[256,4,128]{2,1,0:T(4,128)} %bitcast.7, bf16[512,1536]{1,0:T(8,128)(2,1)} %stem_hbm.1, f32[1,1536]{1,0:T(1,128)} %gain_hbm.1, f32[5,1,1536]{2,1,0:T(1,128)} %bitcast.8, bf16[1,1536,1536]{2,1,0:T(8,128)(2,1)} %weight_hbm.1, s32[1,32]{1,0:T(1,128)} %bitcast.9), custom_call_target="tpu_custom_call" | custom-call | tf_op jit(solution)/shard_map/pallas_call | solution.py:353
  103.3 3.8 %copy.8 = bf16[1,4,256,1536]{3,2,1,0:T(8,128)(2,1)} copy(bf16[1,4,256,1536]{3,2,1,0:T(8,128)(2,1)} %bitcast.6) | data formatting | bytes 6291456

commit v3 on v2

--- a/solution.py
+++ b/solution.py
@@ -94,6 +94,35 @@
     state_buf[CHUNK : CHUNK + LEAD] = jnp.zeros((LEAD, channels), jnp.float32)
     normed_buf[CHUNK : CHUNK + LEAD] = jnp.zeros((LEAD, channels), jnp.float32)
 
+    iota = functools.partial(lax.broadcasted_iota, jnp.int32)
+
+    def zero_one(flags):
+        return jnp.where(flags, 1.0, 0.0).astype(jnp.bfloat16)
+
+    def build_order():
+        dest_row = dest_ref[...]
+        slot = lax.div(dest_row, segs_dev) * per_peer + lax.rem(
+            lax.rem(dest_row, segs_dev), per_peer
+        )
+        runs = zero_one(iota((segs_dev, segs_dev), 0) == slot)
+        by_slot = zero_one(
+            lax.div(iota((rows, segs_dev), 0), seg_rows) == iota((rows, segs_dev), 1)
+        )
+        lag = halo + reach * (sec + 1)
+        source = iota((segs_dev, span), 1) - lag
+        by_run = zero_one(
+            (source >= 0)
+            & (lax.div(jnp.maximum(source, 0), seg_rows) == iota((segs_dev, span), 0))
+        )
+        picked = jnp.dot(by_slot, runs, preferred_element_type=jnp.float32).astype(jnp.bfloat16)
+        picked = jnp.dot(picked, by_run, preferred_element_type=jnp.float32)
+        phase = lax.rem(
+            iota((rows, span), 0) - iota((rows, span), 1) + (lag + seg_rows * span), seg_rows
+        )
+        order_ref[...] = jnp.where(phase == 0, picked, 0.0).astype(jnp.bfloat16)
+
+    build_order()
+
     @pl.when(last)
     def _():
         pl.semaphore_wait(barrier, peers - 1)
@@ -156,33 +185,6 @@
             for m in range(micro):
                 to_left(m).wait_send()
                 to_right(m).wait_recv()
-
-    iota = functools.partial(lax.broadcasted_iota, jnp.int32)
-
-    def zero_one(flags):
-        return jnp.where(flags, 1.0, 0.0).astype(jnp.bfloat16)
-
-    def build_order():
-        dest_row = dest_ref[...]
-        slot = lax.div(dest_row, segs_dev) * per_peer + lax.rem(
-            lax.rem(dest_row, segs_dev), per_peer
-        )
-        runs = zero_one(iota((segs_dev, segs_dev), 0) == slot)
-        by_slot = zero_one(
-            lax.div(iota((rows, segs_dev), 0), seg_rows) == iota((rows, segs_dev), 1)
-        )
-        lag = halo + reach * (sec + 1)
-        source = iota((segs_dev, span), 1) - lag
-        by_run = zero_one(
-            (source >= 0)
-            & (lax.div(jnp.maximum(source, 0), seg_rows) == iota((segs_dev, span), 0))
-        )
-        picked = jnp.dot(by_slot, runs, preferred_element_type=jnp.float32).astype(jnp.bfloat16)
-        picked = jnp.dot(picked, by_run, preferred_element_type=jnp.float32)
-        phase = lax.rem(
-            iota((rows, span), 0) - iota((rows, span), 1) + (lag + seg_rows * span), seg_rows
-        )
-        order_ref[...] = jnp.where(phase == 0, picked, 0.0).astype(jnp.bfloat16)
 
     def state_copy(i):
         part = pl.ds(pl.multiple_of(i * CHUNK, CHUNK), CHUNK)
@@ -307,7 +309,6 @@
 
         return carry
 
-    build_order()
     for load in loads:
         load.wait()
     lax.fori_loop(0, chunks, step, 0)

time: 107 us -> 107 us (level)
  no operation moved by 1% of the time
where the time goes in v3:
time: 107 us
  Pallas kernels  103 us (96%)
  local copies, waits for them, and re-layouts  3.76 us (4%)
    pallas_call x1, Pallas kernels, on_device(): pl.pallas_call(functools.partial(kernel, (micro, rows, halo, sections, pe...  103 us
    unnamed x1, local copies, waits for them, and re-layouts  3.76 us

profile of v3, /device:TPU:25, one launch (start us, length us, event | category | flops | bytes accessed | tf_op | source)
XLA Modules:
  0.0 106.7 jit_solution(12130250893736160434)
XLA Ops:
  0.0 102.9 %shard_map.64 = bf16[4,8,32,1536]{3,2,1,0:T(8,128)(2,1)} custom-call(s32[256,4,128]{2,1,0:T(4,128)} %bitcast.7, bf16[512,1536]{1,0:T(8,128)(2,1)} %stem_hbm.1, f32[1,1536]{1,0:T(1,128)} %gain_hbm.1, f32[5,1,1536]{2,1,0:T(1,128)} %bitcast.8, bf16[1,1536,1536]{2,1,0:T(8,128)(2,1)} %weight_hbm.1, s32[1,32]{1,0:T(1,128)} %bitcast.9), custom_call_target="tpu_custom_call" | custom-call | tf_op jit(solution)/shard_map/pallas_call | solution.py:354
  102.9 3.8 %copy.8 = bf16[1,4,256,1536]{3,2,1,0:T(8,128)(2,1)} copy(bf16[1,4,256,1536]{3,2,1,0:T(8,128)(2,1)} %bitcast.6) | data formatting | bytes 6291456
